TPU v7x, 128 devices: a whole 4x4x4 slice. The times are simulated.
128 devices in a mesh: lat: 16 (over z, x_hi, core), lon: 8 (over x_lo, y).
Axes of the slice: x: 4 (x_hi: 2, x_lo: 2; x = x_hi * 2 + x_lo), y: 4, z: 4, core: 2. Of those that a mesh axis runs over, the one named last changes fastest.
Arguments:
- grid_feat: bfloat16 [32, 16, 128, 474], P('lat', 'lon'), may hold values from -40 to 40
- mesh_feat: bfloat16 [16, 8, 3, 384], P('lat', 'lon'), may hold values from -1 to 1
- g2m_feat: bfloat16 [16, 8, 6, 4, 128], P('lat', 'lon'), may hold values from -4 to 4
- g2m_src: int32 [16, 8, 6], P('lat', 'lon'), may hold values from 0 to 15
- g2m_dst: int32 [16, 8, 6], P('lat', 'lon'), may hold values from 0 to 2
- g2m_rows: int32 [16, 8, 6, 2, 128], P('lat', 'lon'), may hold values from 0 to 127
- g2m_mask: int32 [16, 8, 6, 128], P('lat', 'lon'), may hold values 0 or 1
- g2m_live: int32 [16, 8], P('lat', 'lon'), may hold values from 1 to 6, as said below
- mesh_efeat: bfloat16 [16, 8, 24, 4, 128], P('lat', 'lon'), may hold values from -4 to 4
- mesh_src: int32 [16, 8, 24], P('lat', 'lon'), may hold values from 0 to 34
- mesh_dst: int32 [16, 8, 24], P('lat', 'lon'), may hold values from 0 to 2
- mesh_rows: int32 [16, 8, 24, 2, 128], P('lat', 'lon'), may hold values from 0 to 127
- mesh_mask: int32 [16, 8, 24, 128], P('lat', 'lon'), may hold values 0 or 1
- grid_in: bfloat16 [474, 512], replicated, may hold values from -0.25 to 0.25
- mesh_in: bfloat16 [3, 512], replicated, may hold values from -3.5 to 3.5
- edge_in: bfloat16 [2, 4, 512], replicated, may hold values from -3 to 3
- edge_first: bfloat16 [2, 1536, 512], replicated, may hold values from -0.15625 to 0.15625
- node_first: bfloat16 [2, 1024, 512], replicated, may hold values from -0.1875 to 0.1875
- second: bfloat16 [8, 512, 512], replicated, may hold values from -0.25 to 0.25
- norm_gains: bfloat16 [8, 512], replicated, may hold values from 0.099609375 to 1.8984375
Outputs:
- mesh_out: bfloat16 [16, 8, 384, 512], P('lat', 'lon')
Inputs may be any that keep to these rules, and one draw needn't show every extreme that they name: `g2m_live`: the bands at both poles have all 6 block pairs live.
All inputs are finite; a program needn't handle non-finite values. No bound on the sum of `g2m_mask` or of `mesh_mask` on one device may be relied on, other than what follows from the above.
Results may differ from a plain program's by a relative error of at most 0.015.
Values may be sent and summed in bfloat16 or wider, within the bound.
A program may use at most 64 MiB of HBM per device.

v0:
```python
import jax
import jax.numpy as jnp
from jax import lax
from jax.sharding import PartitionSpec as P

COARSE_DEV = 8


def extended(block, sides, width, periodic):
    for axis, dim in sides:
        count = lax.axis_size(axis)
        forward = [(i, i + 1) for i in range(count - 1)]
        if periodic:
            forward.append((count - 1, 0))
        backward = [(target, source) for source, target in forward]
        low = lax.ppermute(
            lax.slice_in_dim(block, block.shape[dim] - width, None, axis=dim), axis, forward
        )
        high = lax.ppermute(lax.slice_in_dim(block, 0, width, axis=dim), axis, backward)
        block = jnp.concatenate([low, block, high], axis=dim)
    return block


def perceptron(inputs, first_weight, second_weight, gain_row):
    hidden = jax.nn.silu(jnp.dot(inputs, first_weight, preferred_element_type=jnp.float32)).astype(
        jnp.bfloat16
    )
    outputs = jnp.dot(hidden, second_weight, preferred_element_type=jnp.float32)
    centred = outputs - jnp.mean(outputs, axis=-1, keepdims=True)
    spread = jnp.mean(centred * centred, axis=-1, keepdims=True)
    return centred * lax.rsqrt(spread + 1e-05) * gain_row.astype(jnp.float32)


def block_messages(
    source_block,
    target_block,
    features,
    row_pair,
    weighting,
    edge_weight,
    update_weight,
    embed_second,
    embed_gain,
    update_second,
    update_gain,
):
    positions = jnp.arange(source_block.shape[0], dtype=jnp.int32)
    pick_source = (row_pair[0][:, None] == positions[None, :]).astype(jnp.bfloat16)
    pick_target = (row_pair[1][:, None] == positions[None, :]).astype(jnp.bfloat16)
    edge_start = perceptron(features.T, edge_weight, embed_second, embed_gain).astype(jnp.bfloat16)
    source_rows = jnp.dot(pick_source, source_block, preferred_element_type=jnp.float32).astype(
        jnp.bfloat16
    )
    target_rows = jnp.dot(pick_target, target_block, preferred_element_type=jnp.float32).astype(
        jnp.bfloat16
    )
    joined = jnp.concatenate([edge_start, source_rows, target_rows], axis=1)
    updated = edge_start.astype(jnp.float32) + perceptron(
        joined, update_weight, update_second, update_gain
    )
    message = (updated * weighting[:, None]).astype(jnp.bfloat16)
    return jnp.dot(pick_target.T, message, preferred_element_type=jnp.float32)


def per_device(
    grid_feat,
    mesh_feat,
    g2m_feat,
    g2m_src,
    g2m_dst,
    g2m_rows,
    g2m_mask,
    g2m_live,
    mesh_efeat,
    mesh_src,
    mesh_dst,
    mesh_rows,
    mesh_mask,
    grid_in,
    mesh_in,
    edge_in,
    edge_first,
    node_first,
    second,
    norm_gains,
):
    width = second.shape[-1]
    block_rows = grid_feat.shape[2]
    own_tile = perceptron(grid_feat, grid_in, second[0], norm_gains[0]).astype(jnp.bfloat16)
    lon_wide = extended(own_tile, (("lon", 1),), 1, True)
    grid_wide = extended(lon_wide, (("lat", 0),), 1, False)
    grid_table = grid_wide.reshape(-1, block_rows, width)
    mesh_start = perceptron(
        jnp.swapaxes(mesh_feat[0, 0], 0, 1), mesh_in, second[1], norm_gains[1]
    ).astype(jnp.bfloat16)
    start_blocks = mesh_start.reshape(-1, block_rows, width)
    target_count = start_blocks.shape[0]
    g2m_features = g2m_feat[0, 0]
    g2m_sources = g2m_src[0, 0]
    g2m_targets = g2m_dst[0, 0]
    g2m_pairs = g2m_rows[0, 0]
    g2m_weights = g2m_mask[0, 0]
    live_count = g2m_live[0, 0]
    empty_sum = jnp.zeros((target_count, block_rows, width), jnp.float32)

    def g2m_block(source_block, target_block, features, row_pair, weighting):
        return block_messages(
            source_block,
            target_block,
            features,
            row_pair,
            weighting,
            edge_in[0],
            edge_first[0],
            second[2],
            norm_gains[2],
            second[4],
            norm_gains[4],
        )

    def add_local(slot_index, running):
        block_sum = g2m_block(
            grid_table[g2m_sources[slot_index]],
            start_blocks[g2m_targets[slot_index]],
            g2m_features[slot_index],
            g2m_pairs[slot_index],
            g2m_weights[slot_index].astype(jnp.float32),
        )
        return running.at[g2m_targets[slot_index]].add(block_sum)

    g2m_sum = lax.fori_loop(jnp.int32(0), live_count, add_local, empty_sum)
    g2m_round = g2m_sum.reshape(-1, width).astype(jnp.bfloat16)
    mesh_one = (
        mesh_start.astype(jnp.float32)
        + perceptron(
            jnp.concatenate([mesh_start, g2m_round], axis=1),
            node_first[0],
            second[6],
            norm_gains[6],
        )
    ).astype(jnp.bfloat16)
    own_patch = mesh_one.reshape(1, 1, -1, width)
    lon_patches = extended(own_patch, (("lon", 1),), 1, True)
    near_patches = extended(lon_patches, (("lat", 0),), 1, False)
    coarse_all = lax.all_gather(mesh_one[:COARSE_DEV], ("lat", "lon"), axis=0, tiled=True)
    mesh_table = jnp.concatenate(
        [near_patches.reshape(-1, block_rows, width), coarse_all.reshape(-1, block_rows, width)],
        axis=0,
    )
    one_blocks = mesh_one.reshape(-1, block_rows, width)

    def add_mesh(slot_index, running):
        target_index = mesh_dst[0, 0, slot_index]
        block_sum = block_messages(
            mesh_table[mesh_src[0, 0, slot_index]],
            one_blocks[target_index],
            mesh_efeat[0, 0, slot_index],
            mesh_rows[0, 0, slot_index],
            mesh_mask[0, 0, slot_index].astype(jnp.float32),
            edge_in[1],
            edge_first[1],
            second[3],
            norm_gains[3],
            second[5],
            norm_gains[5],
        )
        return running.at[target_index].add(block_sum)

    mesh_sum = lax.fori_loop(jnp.int32(0), jnp.int32(mesh_src.shape[2]), add_mesh, empty_sum)
    mesh_round = mesh_sum.reshape(-1, width).astype(jnp.bfloat16)
    result_rows = (
        mesh_one.astype(jnp.float32)
        + perceptron(
            jnp.concatenate([mesh_one, mesh_round], axis=1), node_first[1], second[7], norm_gains[7]
        )
    ).astype(jnp.bfloat16)
    return result_rows.reshape(1, 1, -1, width)


def solution(mesh):
    in_specs = (
        P("lat", "lon", None, None),
        P("lat", "lon", None, None),
        P("lat", "lon", None, None, None),
        P("lat", "lon", None),
        P("lat", "lon", None),
        P("lat", "lon", None, None, None),
        P("lat", "lon", None, None),
        P("lat", "lon"),
        P("lat", "lon", None, None, None),
        P("lat", "lon", None),
        P("lat", "lon", None),
        P("lat", "lon", None, None, None),
        P("lat", "lon", None, None),
        P(),
        P(),
        P(),
        P(),
        P(),
        P(),
        P(),
    )
    out_specs = P("lat", "lon", None, None)
    return jax.shard_map(
        per_device, mesh=mesh, in_specs=in_specs, out_specs=out_specs, check_vma=False
    )
```

profile of v0, /device:TPU:1, one launch (start us, length us, event | category | flops | bytes accessed | tf_op | source)
XLA Modules:
  0.0 735.0 jit_solution(4797301369545176746)
XLA Ops:
  10.3 2.2 collective-permute-start
  12.5 2.4 collective-permute-start.1
  16.7 4.1 collective-permute-done
  21.8 5.8 collective-permute-start.2
  30.0 4.0 collective-permute-done.2
  34.0 7.7 %collective-permute-done.3 = bf16[1,4,128,512]{3,2,1,0:T(8,128)(2,1)} collective-permute-done((bf16[1,4,128,512]{3,2,1,0:T(8,128)(2,1)S(1)}, bf16[1,4,128,512]{3,2,1,0:T(8,128)(2,1)}, u32[]{:S(2)}, u32[]{:S(2)}) %collective-permute-start.3) | collective-permute-done | bytes 524320 | tf_op jit(solution)/shard_map/ppermute | solution.py:19
  41.7 2.8 pad_maximum_fusion.2
  44.7 55.0 %while.22 = (s32[]{:T(128)}, f32[3,128,512]{2,1,0:T(8,128)S(1)}, s32[]{:T(128)}, s32[6]{0:T(128)S(1)}, s32[6,2,128]{2,1,0:T(2,128)}, /*index=5*/bf16[6,4,128]{2,...) while((s32[]{:T(128)}, f32[3,128,512]{2,1,0:T(8,128)S(1)}, ...), condition=%wide.region_10.11_spmd, body=%wide.region_4.10_spmd.sunk | while | flops 389793184 | bytes 5930345 | solution.py:131
  100.4 2.5 fusion.195
  103.5 14.0 %collective-permute-start.4 = (bf16[1,1,384,512]{3,2,1,0:T(8,128)(2,1)S(1)}, bf16[1,1,384,512]{3,2,1,0:T(8,128)(2,1)S(1)}, u32[]{:S(2)}, u32[]{:S(2)}) collective-permute-start(bf16[1,1,384,512]{3,2,1,0:T(8,128)(2,1)S(1)} %bitcast.252), channel_id=1, source_target_pairs={{0,1},{1,2},{2,3},{3,4},{4,5},{5,6},{6,7},{7,0},{8,9},{9,10},{10,1... | collective-permute-start | bytes 1179656 | tf_op jit(solution)/shard_map/ppermute | solution.py:16
  117.5 3.4 collective-permute-start.5
  121.5 5.2 collective-permute-done.4
  129.8 5.6 collective-permute-start.7
  135.3 8.1 %collective-permute-done.6 = bf16[1,3,384,512]{3,2,1,0:T(8,128)(2,1)S(1)} collective-permute-done((bf16[1,3,384,512]{3,2,1,0:T(8,128)(2,1)}, bf16[1,3,384,512]{3,2,1,0:T(8,128)(2,1)S(1)}, u32[]{:S(2)}, u32[]{:S(2)}) %collective-permute-start.6) | collective-permute-done | bytes 1179680 | tf_op jit(solution)/shard_map/ppermute | solution.py:16
  143.5 5.9 collective-permute-done.7
  149.4 3.1 pad_maximum_fusion.1
  152.4 256.1 %all-gather.2.cloned.1.call-done = bf16[1024,512]{1,0:T(8,128)(2,1)} async-done(((bf16[8,512]{1,0:T(8,128)(2,1)}), bf16[1024,512]{1,0:T(8,128)(2,1)}) %all-gather.2.cloned.1.call-update) | async-done | bytes 1048592 | tf_op jit(solution)/shard_map/all_gather | solution.py:145
  408.5 4.8 pad_maximum_fusion
  413.4 311.0 %while.23 = (s32[]{:T(128)}, f32[3,128,512]{2,1,0:T(8,128)S(1)}, s32[1,1,24]{2,1,0:T(1,128)S(1)}, s32[1,1,24,2,128]{4,3,2,1,0:T(2,128)}, bf16[1,1,24,4,128]{4,3,...) while((s32[]{:T(128)}, f32[3,128,512]{2,1,0:T(8,128)S(1)}, ...), condition=%wide.region_19.20_spmd, body=%wide.region_13.19_spmd.sunk | while | flops 389793184 | bytes 5930799 | solution.py:169
  434.5 2.2 fusion.243
  447.5 2.2 fusion.243
  473.4 2.2 fusion.243
  499.3 2.2 fusion.243
  525.3 2.2 fusion.243
  551.2 2.2 fusion.243
  577.1 2.2 fusion.243
  603.0 2.2 fusion.243
  628.9 2.2 fusion.243
  654.9 2.2 fusion.243
  680.8 2.2 fusion.243
  706.7 2.2 fusion.243
  724.5 2.4 fusion.200
  (553 shorter events, 247.3 us)
Async XLA Ops:
  6.5 1.0 copy-start
  6.5 3.5 copy-start.1
  6.5 402.0 %all-gather.2.cloned.1.call-start = ((), (), s32[]{:S(2)}) async-start(), calls=%async_computation | async-start | bytes 1056768 | tf_op jit(solution)/shard_map/all_gather | solution.py:145
  9.7 5.2 copy-start.7
  9.7 5.2 copy-start.8
  10.3 10.5 %collective-permute-start = (bf16[2,1,128,512]{3,2,1,0:T(8,128)(2,1)S(1)}, bf16[2,1,128,512]{3,2,1,0:T(8,128)(2,1)S(1)}, u32[]{:S(2)}, u32[]{:S(2)}) collective-permute-start(bf16[2,1,128,512]{3,2,1,0:T(8,128)(2,1)S(1)} %get-tuple-element.245), channel_id=1, source_target_pairs={{0,1},{1,2},{2,3},{3,4},{4,5},{5,6},{6,7},{7,0},{8,9},{9,10},{10,1... | collective-permute-start | bytes 786440 | tf_op jit(solution)/shard_map/ppermute | solution.py:16
  12.5 8.3 %collective-permute-start.1 = (bf16[2,1,128,512]{3,2,1,0:T(8,128)(2,1)S(1)}, bf16[2,1,128,512]{3,2,1,0:T(8,128)(2,1)S(1)}, u32[]{:S(2)}, u32[]{:S(2)}) collective-permute-start(bf16[2,1,128,512]{3,2,1,0:T(8,128)(2,1)S(1)} %get-tuple-element.246), channel_id=1, source_target_pairs={{1,0},{2,1},{3,2},{4,3},{5,4},{6,5},{7,6},{0,7},{9,8},{10,9},{11,1... | collective-permute-start | bytes 786440 | tf_op jit(solution)/shard_map/ppermute | solution.py:19
  16.7 13.0 %copy-start.5 = (s32[1,1,6,128]{3,1,2,0:T(1,128)S(1)}, s32[1,1,6,128]{3,1,2,0:T(1,128)}, u32[]{:S(2)}) copy-start(s32[1,1,6,128]{3,1,2,0:T(1,128)} %param.34) | copy-start | bytes 9220
  21.8 12.2 %collective-permute-start.2 = (bf16[1,4,128,512]{3,2,1,0:T(8,128)(2,1)}, bf16[1,4,128,512]{3,2,1,0:T(8,128)(2,1)}, u32[]{:S(2)}, u32[]{:S(2)}) collective-permute-start(bf16[1,4,128,512]{3,2,1,0:T(8,128)(2,1)} %get-tuple-element.243), channel_id=1, source_target_pairs={{0,8},{8,16},{16,24},{24,32},{32,40},{40,48},{48,56},{56,64},{64,7... | collective-permute-start | bytes 1572872 | tf_op jit(solution)/shard_map/ppermute | solution.py:16
  27.6 14.1 %collective-permute-start.3 = (bf16[1,4,128,512]{3,2,1,0:T(8,128)(2,1)S(1)}, bf16[1,4,128,512]{3,2,1,0:T(8,128)(2,1)}, u32[]{:S(2)}, u32[]{:S(2)}) collective-permute-start(bf16[1,4,128,512]{3,2,1,0:T(8,128)(2,1)S(1)} %get-tuple-element.244), channel_id=1, source_target_pairs={{8,0},{16,8},{24,16},{32,24},{40,32},{48,40},{56,48},{64,56},{72,6... | collective-permute-start | bytes 1572872 | tf_op jit(solution)/shard_map/ppermute | solution.py:19
  29.7 14.9 %copy-start.2 = (s32[3]{0:T(128)S(1)}, s32[3]{0:T(128)}, u32[]{:S(2)}) copy-start(s32[3]{0:T(128)} %constant.97.clone.1) | copy-start | bytes 40
  29.8 14.9 %copy-start.6 = (bf16[2,4,512]{2,1,0:T(4,128)(2,1)S(1)}, bf16[2,4,512]{2,1,0:T(4,128)(2,1)}, u32[]{:S(2)}) copy-start(bf16[2,4,512]{2,1,0:T(4,128)(2,1)} %param.43) | copy-start | bytes 24580
  29.8 14.9 %copy-start.9 = (s32[1,1,6]{2,1,0:T(1,128)S(1)}, s32[1,1,6]{2,1,0:T(1,128)}, u32[]{:S(2)}) copy-start(s32[1,1,6]{2,1,0:T(1,128)} %param.32) | copy-start | bytes 76
  29.8 14.9 %copy-start.10 = (s32[1,1,6]{2,1,0:T(1,128)S(1)}, s32[1,1,6]{2,1,0:T(1,128)}, u32[]{:S(2)}) copy-start(s32[1,1,6]{2,1,0:T(1,128)} %param.31) | copy-start | bytes 76
  103.5 23.2 %collective-permute-start.4 = (bf16[1,1,384,512]{3,2,1,0:T(8,128)(2,1)S(1)}, bf16[1,1,384,512]{3,2,1,0:T(8,128)(2,1)S(1)}, u32[]{:S(2)}, u32[]{:S(2)}) collective-permute-start(bf16[1,1,384,512]{3,2,1,0:T(8,128)(2,1)S(1)} %bitcast.252), channel_id=1, source_target_pairs={{0,1},{1,2},{2,3},{3,4},{4,5},{5,6},{6,7},{7,0},{8,9},{9,10},{10,1... | collective-permute-start | bytes 1179656 | tf_op jit(solution)/shard_map/ppermute | solution.py:16
  117.5 9.1 %collective-permute-start.5 = (bf16[1,1,384,512]{3,2,1,0:T(8,128)(2,1)S(1)}, bf16[1,1,384,512]{3,2,1,0:T(8,128)(2,1)S(1)}, u32[]{:S(2)}, u32[]{:S(2)}) collective-permute-start(bf16[1,1,384,512]{3,2,1,0:T(8,128)(2,1)S(1)} %bitcast.253), channel_id=1, source_target_pairs={{1,0},{2,1},{3,2},{4,3},{5,4},{6,5},{7,6},{0,7},{9,8},{10,9},{11,1... | collective-permute-start | bytes 1179656 | tf_op jit(solution)/shard_map/ppermute | solution.py:19
  127.9 15.6 %collective-permute-start.6 = (bf16[1,3,384,512]{3,2,1,0:T(8,128)(2,1)}, bf16[1,3,384,512]{3,2,1,0:T(8,128)(2,1)S(1)}, u32[]{:S(2)}, u32[]{:S(2)}) collective-permute-start(bf16[1,3,384,512]{3,2,1,0:T(8,128)(2,1)} %pad_maximum_fusion.3), channel_id=1, source_target_pairs={{0,8},{8,16},{16,24},{24,32},{32,40},{40,48},{48,56},{56,64},{64,7... | collective-permute-start | bytes 3538952 | tf_op jit(solution)/shard_map/ppermute | solution.py:16
  129.8 19.6 %collective-permute-start.7 = (bf16[1,3,384,512]{3,2,1,0:T(8,128)(2,1)}, bf16[1,3,384,512]{3,2,1,0:T(8,128)(2,1)}, u32[]{:S(2)}, u32[]{:S(2)}) collective-permute-start(bf16[1,3,384,512]{3,2,1,0:T(8,128)(2,1)} %pad_maximum_fusion.3), channel_id=1, source_target_pairs={{8,0},{16,8},{24,16},{32,24},{40,32},{48,40},{56,48},{64,56},{72,6... | collective-permute-start | bytes 3538952 | tf_op jit(solution)/shard_map/ppermute | solution.py:19
  408.5 4.9 copy-start.3
  408.5 4.9 copy-start.4
Sparse Core Ops, SparseCore 0:
  121.6 286.8 all-gather.1
where the time goes:
time: 741 us; the launch traced here: 735 us
  waiting for transfers between devices  291 us (39%)
  matrix products  177 us (24%)
  loops' own time  108 us (15%)
  other arithmetic  66.5 us (9%)
  local copies, waits for them, and re-layouts  41.2 us (6%)
  starting transfers between devices  37.2 us (5%)
  between operations  13.7 us (2%)
    all_gather x1, waiting for transfers between devices, per_device(): lax.all_gather(mesh_one[:COARSE_DEV], ('lat', 'lon'), axis=0, tiled=True)  256 us
    dot_general x60, matrix products, perceptron(): outputs = jnp.dot(hidden, second_weight, preferred_element_type=jnp.float32)  113 us
    another operation x1, loops' own time, per_device(): lax.fori_loop(jnp.int32(0), jnp.int32(mesh_src.shape[2]), add_mesh, empty...  89.6 us
    dot_general x28, matrix products, block_messages(): jnp.dot(pick_source, source_block, preferred_element_type=jnp.float32)  31.6 us
    dot_general x28, matrix products, block_messages(): return jnp.dot(pick_target.T, message, preferred_element_type=jnp.float32)  26.6 us
    ppermute x4, starting transfers between devices, extended(): lax.ppermute(lax.slice_in_dim(block, block.shape[dim] - width, None, axis...  23.9 us
    ppermute x4, waiting for transfers between devices, extended(): lax.ppermute(lax.slice_in_dim(block, block.shape[dim] - width, None, axis...  21.3 us
    another operation x28, other arithmetic  20.3 us
  transfers between devices with their start and end apart: 9, of which 7 were waited for; matrix products, arithmetic and copies ran while one was open for 1% of the time, Pallas kernels for 0%

commit v1 on v0

v1 whole, which is shorter than its diff:
```python
import functools

import jax
import jax.numpy as jnp
from jax import lax
from jax.experimental import pallas as pl
from jax.experimental.pallas import tpu as pltpu
from jax.sharding import PartitionSpec as P

BF = jnp.bfloat16
F32 = jnp.float32
MESH = pl.DeviceIdType.MESH
BLK = 128
GROUP = 4
GGROUP = 3
EARLY = 2
NEAR = 27
COARSE = 8


def mm(a, b):
    return jnp.dot(a, b, preferred_element_type=F32)


def silu(x):
    half = 0.5 * x
    return (half * jnp.tanh(half) + half).astype(BF)


def unit_rows(v):
    return v * lax.rsqrt(jnp.mean(v * v, axis=-1, keepdims=True) + 1e-05)


def kernel(
    grid_feat,
    grid_in,
    second,
    edge_first,
    node_first,
    mesh_feat,
    g2m_feat,
    g2m_rows,
    g2m_mask,
    mesh_efeat,
    mesh_rows,
    mesh_mask,
    mesh_in,
    edge_in,
    norm_gains,
    g2m_src,
    g2m_dst,
    g2m_live,
    mesh_src,
    mesh_dst,
    out,
    feat_v,
    gin_v,
    sec_v,
    ef_v,
    nf_v,
    gt,
    mt,
    start_v,
    one_v,
    dproj,
    npre,
    g_pre,
    g_pick,
    g_scat,
    m_pre,
    m_pick,
    m_scat,
    acc_e,
    acc_m,
    acc_g,
    acc_h,
    load_sem,
    send_sem,
    recv_sem,
):
    lat, lon = lax.axis_index("lat"), lax.axis_index("lon")
    n_lat, n_lon = lax.axis_size("lat"), lax.axis_size("lon")
    par = lax.rem(lat, 2)
    chip = lat // 2
    east = (lat, lax.rem(lon + 1, n_lon))
    west = (lat, lax.rem(lon + n_lon - 1, n_lon))
    twin = (lat + 1 - 2 * par, lon)
    far_lat = lat + 2 * par - 1
    has_far = jnp.logical_and(far_lat >= 0, far_lat < n_lat)
    far = (far_lat, lon)
    lon_mates = [(lat, lax.rem(lon + t, n_lon)) for t in range(1, n_lon)]
    x_mate = (lat + 2 - 4 * lax.rem(chip, 2), lon)
    z_mates = [(lax.rem(lat + 4 * t, n_lat), lon) for t in range(1, n_lat // 4)]

    loads = {}

    def load(name, src, dst):
        copy = pltpu.make_async_copy(src, dst, load_sem.at[len(loads)])
        copy.start()
        loads[name] = copy

    def loaded(*names):
        for name in names:
            loads[name].wait()

    load("feat", grid_feat, feat_v)
    load("gin", grid_in, gin_v)
    load("s0", second.at[0], sec_v.at[0])
    load("e0", edge_first.at[0], ef_v.at[0])
    load("s1", second.at[1], sec_v.at[1])
    load("s2", second.at[2], sec_v.at[2])
    load("n0", node_first.at[0], nf_v.at[0])
    load("s3", second.at[3], sec_v.at[3])
    load("e1", edge_first.at[1], ef_v.at[1])
    load("s4", second.at[4], sec_v.at[4])
    load("s6", second.at[6], sec_v.at[6])
    load("s5", second.at[5], sec_v.at[5])
    load("n1", node_first.at[1], nf_v.at[1])
    load("s7", second.at[7], sec_v.at[7])

    barrier = pltpu.get_barrier_semaphore()
    mates = lon_mates + [twin, x_mate] + z_mates
    for mate in mates:
        pl.semaphore_signal(barrier, inc=1, device_id=mate, device_id_type=MESH)

    @pl.when(has_far)
    def _():
        pl.semaphore_signal(barrier, inc=1, device_id=far, device_id_type=MESH)

    gains = norm_gains[...].astype(F32)

    def gain(k):
        return gains[k : k + 1]

    def centre(k):
        w = sec_v[k].astype(F32)
        sec_v[k] = (w - jnp.mean(w, axis=-1, keepdims=True)).astype(BF)

    numbers = {}

    def remote(name, src, dst, device):
        index = numbers.setdefault(name, len(numbers))
        return pltpu.make_async_remote_copy(
            src_ref=src,
            dst_ref=dst,
            send_sem=send_sem.at[index],
            recv_sem=recv_sem.at[index],
            device_id=device,
            device_id_type=MESH,
        )

    def g_at(r, c, n=1):
        return gt.at[pl.ds(r * 4 + c, n)]

    on_row, off_row = 3 * (1 - par), 3 * par
    g_rows = (1 + par, 2 - par)
    g_copies = {}
    for t in range(2):
        g_copies["e", t] = remote(("ge", t), g_at(g_rows[t], 2), g_at(g_rows[t], 0), east)
        g_copies["w", t] = remote(("gw", t), g_at(g_rows[t], 1), g_at(g_rows[t], 3), west)
    g_copies["far"] = remote("gfar", g_at(g_rows[0], 1, 2), g_at(on_row, 1, 2), far)
    g_copies["twin"] = remote("gtwin", g_at(g_rows[1], 1, 2), g_at(off_row, 1, 2), twin)
    g_copies["far_e"] = remote("gfe", g_at(off_row, 2), g_at(off_row, 0), east)
    g_copies["far_w"] = remote("gfw", g_at(off_row, 1), g_at(off_row, 3), west)
    g_copies["twin_e"] = remote("gte", g_at(g_rows[1], 0), g_at(off_row, 0), twin)
    g_copies["twin_w"] = remote("gtw", g_at(g_rows[1], 3), g_at(off_row, 3), twin)

    @pl.when(jnp.logical_not(has_far))
    def _():
        gt[pl.ds(off_row * 4, 4)] = jnp.zeros((4, BLK, 512), BF)
        mt[pl.ds(2 * par * 9, 9)] = jnp.zeros((9, BLK, 512), BF)

    loaded("feat", "gin", "s0")
    centre(0)
    w_in = gin_v[...]
    for t in range(2):
        x = feat_v[g_rows[t] - 1].reshape(2 * BLK, -1)
        v = mm(silu(mm(x, w_in)), sec_v[0])
        latent = (unit_rows(v) * gain(0)).astype(BF)
        if t == 0:
            loaded("e0")
        proj = mm(latent, ef_v[0, 512:1024]).astype(BF)
        gt[pl.ds(g_rows[t] * 4 + 1, 2)] = proj.reshape(2, BLK, 512)
        if t == 0:
            pl.semaphore_wait(barrier, len(mates) + jnp.where(has_far, 1, 0))

            @pl.when(has_far)
            def _():
                g_copies["far"].start()

        else:
            g_copies["twin"].start()
        g_copies["e", t].start()
        g_copies["w", t].start()

    loaded("s1")
    centre(1)
    u = lax.dot_general(
        mesh_feat[0, 0], mesh_in[...], (((0,), (0,)), ((), ())), preferred_element_type=F32
    )
    start = (unit_rows(mm(silu(u), sec_v[1])) * gain(1)).astype(BF)
    start_v[...] = start
    dproj[...] = mm(start, ef_v[0, 1024:1536]).astype(BF).reshape(3, BLK, 512)
    loaded("n0")
    npre[...] = mm(start, nf_v[0, 0:512])

    def embed(base, count, feat, rows, mask, src, dst, live, layer, k, pre, pick, scat, acc, far_blocks):
        w_edge = edge_in[layer]
        hidden = []
        scatters = []
        spot = lax.broadcasted_iota(jnp.int32, (BLK, BLK), 0)
        place = lax.broadcasted_iota(jnp.int32, (3 * BLK, BLK), 0)
        for q in range(count):
            s = base + q
            u = lax.dot_general(
                feat[0, 0, s], w_edge, (((0,), (0,)), ((), ())), preferred_element_type=F32
            )
            hidden.append(silu(u))
            pair = rows[0, 0, s]
            hs, hd = pair[0:1], pair[1:2]
            if far_blocks:
                moved = ((hs >> 3) & 7) * 16 + (hs >> 6) * 8 + (hs & 7)
                is_coarse = jnp.where(src[0, 0, s] >= NEAR, 1, 0)
                hs = hs + is_coarse * (moved - hs)
            pick_s = jnp.where(spot == hs, 1.0, 0.0).T.astype(BF)
            pick_d = jnp.where(spot == hd, 1.0, 0.0).T.astype(BF)
            pick[s] = jnp.concatenate([pick_s, pick_d], axis=1)
            keep = mask[0, 0, pl.ds(s, 1), :]
            if live is not None:
                keep = keep * jnp.where(s < live, 1, 0)
            target = jnp.where(keep != 0, hd + BLK * dst[0, 0, s], -1)
            one = jnp.where(place == target, 1.0, 0.0).astype(BF)
            scat[s] = one
            scatters.append(one)
        e = (unit_rows(mm(jnp.concatenate(hidden, axis=0), sec_v[k])) * gain(k)).astype(BF)
        pre[pl.ds(base, count)] = mm(e, ef_v[layer, 0:512]).reshape(count, BLK, 512)
        acc[...] += mm(jnp.concatenate(scatters, axis=1), e)

    def update(base, count, src, dst, k, pre, pick, scat, table, acc):
        hidden = []
        for q in range(count):
            s = base + q
            blocks = jnp.concatenate([table[src[0, 0, s]], dproj[dst[0, 0, s]]], axis=0)
            hidden.append(silu(pre[s] + mm(pick[s], blocks)))
        message = unit_rows(mm(jnp.concatenate(hidden, axis=0), sec_v[k])).astype(BF)
        scatters = jnp.concatenate([scat[base + q] for q in range(count)], axis=1)
        acc[...] += mm(scatters, message)

    zeros = jnp.zeros(acc_e.shape, F32)
    acc_e[...] = zeros
    acc_m[...] = zeros
    acc_g[...] = zeros
    acc_h[...] = zeros
    live = g2m_live[0, 0]
    loaded("s2")
    centre(2)

    @pl.loop(0, 6 // GGROUP)
    def _(n):
        embed(
            n * GGROUP, GGROUP, g2m_feat, g2m_rows, g2m_mask, g2m_src, g2m_dst, live,
            0, 2, g_pre, g_pick, g_scat, acc_g, False,
        )

    @pl.when(has_far)
    def _():
        g_copies["far"].wait_recv()
        g_copies["far_e"].start()
        g_copies["far_w"].start()

    g_copies["e", 1].wait_recv()
    g_copies["twin_e"].start()
    g_copies["w", 1].wait_recv()
    g_copies["twin_w"].start()

    loaded("s3", "e1")
    centre(3)

    def embed_mesh(n):
        embed(
            n * GROUP, GROUP, mesh_efeat, mesh_rows, mesh_mask, mesh_src, mesh_dst, None,
            1, 3, m_pre, m_pick, m_scat, acc_e, True,
        )

    @pl.loop(0, EARLY)
    def _(n):
        embed_mesh(n)

    loaded("s4", "s6", "s5", "s7", "n1")
    for k in (4, 6, 5, 7):
        centre(k)

    for name in (("e", 0), ("w", 0), "twin", "twin_e", "twin_w"):
        g_copies[name].wait_recv()

    @pl.when(has_far)
    def _():
        g_copies["far_e"].wait_recv()
        g_copies["far_w"].wait_recv()

    @pl.loop(0, 6 // GGROUP)
    def _(n):
        update(n * GGROUP, GGROUP, g2m_src, g2m_dst, 4, g_pre, g_pick, g_scat, gt, acc_h)

    def m_at(r, c, b):
        return mt.at[(r * 3 + c) * 3 + b]

    m_on, m_off = 2 * (1 - par), 2 * par
    m_copies = {}
    for b in range(3):
        m_copies["e", b] = remote(("me", b), m_at(1, 1, b), m_at(1, 0, b), east)
        m_copies["w", b] = remote(("mw", b), m_at(1, 1, b), m_at(1, 2, b), west)
        m_copies["far", b] = remote(("mfar", b), m_at(1, 1, b), m_at(m_on, 1, b), far)
        m_copies["twin", b] = remote(("mtwin", b), m_at(1, 1, b), m_at(m_off, 1, b), twin)
        m_copies["far_e", b] = remote(("mfe", b), m_at(m_off, 1, b), m_at(m_off, 0, b), east)
        m_copies["far_w", b] = remote(("mfw", b), m_at(m_off, 1, b), m_at(m_off, 2, b), west)
        m_copies["twin_e", b] = remote(("mte", b), m_at(1, 0, b), m_at(m_off, 0, b), twin)
        m_copies["twin_w", b] = remote(("mtw", b), m_at(1, 2, b), m_at(m_off, 2, b), twin)

    half = pl.ds(pl.multiple_of(par * 256, 256), 256)
    unit = mt.at[NEAR + chip, pl.ds(pl.multiple_of(lon * 16, 16), 16), half]
    c_lon = [remote(("cl", t), unit, unit, mate) for t, mate in enumerate(lon_mates)]
    line = mt.at[NEAR + chip, :, half]
    c_x = remote("cx", line, line, x_mate)
    plane = mt.at[pl.ds(NEAR + 2 * (chip // 2), 2), :, half]
    c_z = [remote(("cz", t), plane, plane, mate) for t, mate in enumerate(z_mates)]
    cube = mt.at[pl.ds(NEAR, 8), :, half]
    c_core = remote("cc", cube, cube, twin)

    g2m_round = (acc_g[...] + acc_h[...] * gain(4)).astype(BF)
    node_w = nf_v[0, 512:1024]
    for b in range(3):
        rows = slice(b * BLK, (b + 1) * BLK)
        u = npre[rows] + mm(g2m_round[rows], node_w)
        step = unit_rows(mm(silu(u), sec_v[6])) * gain(6)
        one = (start_v[rows].astype(F32) + step).astype(BF)
        one_v[rows] = one
        mt[12 + b] = mm(one, ef_v[1, 512:1024]).astype(BF)

        @pl.when(has_far)
        def _(b=b):
            m_copies["far", b].start()

        for name in ("e", "w", "twin"):
            m_copies[name, b].start()

    one = one_v[...]
    dproj[...] = mm(one, ef_v[1, 1024:1536]).astype(BF).reshape(3, BLK, 512)
    m_copies["twin", 0].wait_recv()
    mine = mt[12, 0:16].astype(F32)[0:COARSE]
    other = mt[(m_on * 3 + 1) * 3, 0:16].astype(F32)[0:COARSE]
    top = jnp.where(par == 0, mine, other)
    low = jnp.where(par == 0, other, mine)
    both = jnp.concatenate([top, low], axis=0)
    unit[...] = jnp.where(par == 0, both[:, 0:256], both[:, 256:512]).astype(BF)
    for copy in c_lon:
        copy.start()
    npre[...] = mm(one, nf_v[1, 0:512])

    def forward(b):
        @pl.when(has_far)
        def _():
            m_copies["far", b].wait_recv()
            m_copies["far_e", b].start()
            m_copies["far_w", b].start()

        m_copies["e", b].wait_recv()
        m_copies["twin_e", b].start()
        m_copies["w", b].wait_recv()
        m_copies["twin_w", b].start()

    groups = 24 // GROUP
    late = groups - EARLY

    @pl.loop(EARLY, EARLY + late // 4)
    def _(n):
        embed_mesh(n)

    for copy in c_lon:
        copy.wait_recv()
    c_x.start()
    forward(0)

    @pl.loop(EARLY + late // 4, EARLY + late // 2)
    def _(n):
        embed_mesh(n)

    c_x.wait_recv()
    for copy in c_z:
        copy.start()
    forward(1)

    @pl.loop(EARLY + late // 2, groups)
    def _(n):
        embed_mesh(n)

    forward(2)
    for copy in c_z:
        copy.wait_recv()
    c_core.start()
    for b in range(3):
        if b:
            m_copies["twin", b].wait_recv()
        m_copies["twin_e", b].wait_recv()
        m_copies["twin_w", b].wait_recv()

        @pl.when(has_far)
        def _(b=b):
            m_copies["far_e", b].wait_recv()
            m_copies["far_w", b].wait_recv()

    c_core.wait_recv()

    @pl.loop(0, groups)
    def _(n):
        update(n * GROUP, GROUP, mesh_src, mesh_dst, 5, m_pre, m_pick, m_scat, mt, acc_m)

    mesh_round = (acc_e[...] + acc_m[...] * gain(5)).astype(BF)
    u = npre[...] + mm(mesh_round, nf_v[1, 512:1024])
    step = unit_rows(mm(silu(u), sec_v[7])) * gain(7)
    out[0, 0] = (one_v[...].astype(F32) + step).astype(BF)

    for name, copy in list(g_copies.items()) + list(m_copies.items()):
        kind = name if isinstance(name, str) else name[0]
        if kind.startswith("far"):
            pl.when(has_far)(copy.wait_send)
        else:
            copy.wait_send()
    for copy in c_lon + [c_x] + c_z + [c_core]:
        copy.wait_send()


def per_device(
    grid_feat,
    mesh_feat,
    g2m_feat,
    g2m_src,
    g2m_dst,
    g2m_rows,
    g2m_mask,
    g2m_live,
    mesh_efeat,
    mesh_src,
    mesh_dst,
    mesh_rows,
    mesh_mask,
    grid_in,
    mesh_in,
    edge_in,
    edge_first,
    node_first,
    second,
    norm_gains,
):
    hbm = pl.BlockSpec(memory_space=pl.ANY)
    vmem = pl.BlockSpec(memory_space=pltpu.VMEM)
    smem = pl.BlockSpec(memory_space=pltpu.SMEM)
    copies = 96
    return pl.pallas_call(
        kernel,
        out_shape=jax.ShapeDtypeStruct((1, 1, 384, 512), BF),
        in_specs=[hbm] * 5 + [vmem] * 10 + [smem] * 5,
        out_specs=vmem,
        scratch_shapes=[
            pltpu.VMEM((2, 2, BLK, 474), BF),
            pltpu.VMEM((474, 512), BF),
            pltpu.VMEM((8, 512, 512), BF),
            pltpu.VMEM((2, 1536, 512), BF),
            pltpu.VMEM((2, 1024, 512), BF),
            pltpu.VMEM((16, BLK, 512), BF),
            pltpu.VMEM((NEAR + 8, BLK, 512), BF),
            pltpu.VMEM((384, 512), BF),
            pltpu.VMEM((384, 512), BF),
            pltpu.VMEM((3, BLK, 512), BF),
            pltpu.VMEM((384, 512), F32),
            pltpu.VMEM((6, BLK, 512), F32),
            pltpu.VMEM((6, BLK, 256), BF),
            pltpu.VMEM((6, 384, BLK), BF),
            pltpu.VMEM((24, BLK, 512), F32),
            pltpu.VMEM((24, BLK, 256), BF),
            pltpu.VMEM((24, 384, BLK), BF),
            pltpu.VMEM((384, 512), F32),
            pltpu.VMEM((384, 512), F32),
            pltpu.VMEM((384, 512), F32),
            pltpu.VMEM((384, 512), F32),
            pltpu.SemaphoreType.DMA((14,)),
            pltpu.SemaphoreType.DMA((copies,)),
            pltpu.SemaphoreType.DMA((copies,)),
        ],
        compiler_params=pltpu.CompilerParams(
            collective_id=0, has_side_effects=True, vmem_limit_bytes=56 * 1024 * 1024
        ),
        cost_estimate=pl.CostEstimate(flops=13 * 10**9, bytes_accessed=12 * 2**20, transcendentals=0),
    )(
        grid_feat,
        grid_in,
        second,
        edge_first,
        node_first,
        mesh_feat,
        g2m_feat,
        g2m_rows,
        g2m_mask,
        mesh_efeat,
        mesh_rows,
        mesh_mask,
        mesh_in,
        edge_in,
        norm_gains,
        g2m_src,
        g2m_dst,
        g2m_live,
        mesh_src,
        mesh_dst,
    )


def solution(mesh):
    tile = lambda rank: P("lat", "lon", *([None] * (rank - 2)))
    in_specs = tuple(tile(r) for r in (4, 4, 5, 3, 3, 5, 4, 2, 5, 3, 3, 5, 4)) + (P(),) * 7
    return jax.shard_map(
        per_device, mesh=mesh, in_specs=in_specs, out_specs=tile(4), check_vma=False
    )
```

time: 741 us -> 76.6 us (0.10)
  waiting for transfers between devices: 291 us -> 0 us
  matrix products: 177 us -> 0 us
  loops' own time: 108 us -> 0 us
  Pallas kernels: 0 us -> 70.7 us
  other arithmetic: 66.5 us -> 0 us
  starting transfers between devices: 37.2 us -> 0 us
  local copies, waits for them, and re-layouts: 41.2 us -> 5.02 us
  between operations: 13.7 us -> 0.66 us
    all_gather x1 -> x0, waiting for transfers between devices: 256 us -> none  [per_device(): lax.all_gather(mesh_one[:COARSE_DEV], ('lat', 'lon'), axis=0, tiled=True)]
    dot_general x144 -> x0, matrix products: 177 us -> none  [the longest x60 113 us: perceptron(): outputs = jnp.dot(hidden, second_weight, preferred_element_type=jnp.float32)]
    another operation x2 -> x0, loops' own time: 108 us -> none  [the longest x1 89.6 us: per_device(): lax.fori_loop(jnp.int32(0), jnp.int32(mesh_src.shape[2]), add_mesh, empty...]
    pallas_call x0 -> x1, Pallas kernels: none -> 70.7 us  [per_device(): pl.pallas_call(kernel, out_shape=jax.ShapeDtypeStruct((1, 1, 384, 512), B...]
    dynamic_slice x60 -> x0, local copies, waits for them, and re-layouts: 38.3 us -> none  [the longest x24 16.5 us: add_mesh(): mesh_rows[0, 0, slot_index]]
    ppermute x8 -> x0, starting transfers between devices: 37.2 us -> none  [the longest x4 23.9 us: extended(): lax.ppermute(lax.slice_in_dim(block, block.shape[dim] - width, None, axis...]
    ppermute x8 -> x0, waiting for transfers between devices: 35 us -> none  [the longest x4 21.3 us: extended(): lax.ppermute(lax.slice_in_dim(block, block.shape[dim] - width, None, axis...]
    convert_element_type x61 -> x0, other arithmetic: 21.3 us -> none  [the longest x24 16.6 us: add_mesh(): mesh_mask[0, 0, slot_index].astype(jnp.float32)]
  transfers between devices with their start and end apart: 9 -> 0, of which waited for: 7 -> 0; matrix products, arithmetic and copies ran while one was open for 1% -> 0% of each run, Pallas kernels for 0% -> 0%
where the time goes in v1:
time: 76.6 us; the launch traced here: 76.4 us
  Pallas kernels  70.7 us (92%)
  local copies, waits for them, and re-layouts  5.02 us (7%)
    pallas_call x1, Pallas kernels, per_device(): pl.pallas_call(kernel, out_shape=jax.ShapeDtypeStruct((1, 1, 384, 512), B...  70.7 us
    unnamed x3, local copies, waits for them, and re-layouts  5.02 us

profile of v1, /device:TPU:1, one launch (start us, length us, event | category | flops | bytes accessed | tf_op | source)
XLA Modules:
  0.0 76.4 jit_solution(3156852559883357440)
XLA Ops:
  0.7 1.3 %copy.22.g2m_mask = s32[1,1,6,128]{3,2,1,0:T(8,128)} copy(s32[1,1,6,128]{3,1,2,0:T(1,128)} %param.26) | data formatting | bytes 6144 | tf_op args[6]
  1.9 2.0 %copy.21.grid_feat = bf16[2,2,128,474]{3,2,1,0:T(8,128)(2,1)} copy(bf16[2,2,128,474]{2,1,3,0:T(2,128)(2,1)} %param.20) | data formatting | bytes 970752 | tf_op args[0]
  3.9 70.7 %shard_map.190 = bf16[1,1,384,512]{3,2,1,0:T(8,128)(2,1)} custom-call(bf16[2,2,128,474]{3,2,1,0:T(8,128)(2,1)} %copy.21.grid_feat, bf16[474,512]{1,0:T(8,128)(2,1)} %grid_in.1, bf16[8,512,512]{2,1,0:T(8,128)(2,1)} %second.1, bf16[2,1536,512]{2,1,0:T(8,128)(2,1)} %edge_first.1, bf16[2,1024,512]{2,1,0:T(8,128)(2,1)} %node_first.1, ...), custom_call_target="tpu_custom_call" | custom-call | flops 12999999488 | bytes 12582912 | tf_op jit(solution)/shard_map/pallas_call | solution.py:459
  74.6 1.8 %copy.25 = bf16[1,1,384,512]{3,2,1,0:T(8,128)(2,1)} copy(bf16[1,1,384,512]{3,2,1,0:T(8,128)(2,1)} %shard_map.190) | data formatting | bytes 786432

commit v2 on v1

--- a/solution.py
+++ b/solution.py
@@ -12,7 +12,8 @@
 MESH = pl.DeviceIdType.MESH
 BLK = 128
 GROUP = 4
-GGROUP = 3
+UGROUP = 8
+GGROUP = 6
 EARLY = 2
 NEAR = 27
 COARSE = 8
@@ -37,6 +38,22 @@
     second,
     edge_first,
     node_first,
+    mesh_feat_h,
+    g2m_feat_h,
+    g2m_rows_h,
+    g2m_mask_h,
+    mesh_efeat_h,
+    mesh_rows_h,
+    mesh_mask_h,
+    mesh_in_h,
+    edge_in_h,
+    norm_gains_h,
+    g2m_src_h,
+    g2m_dst_h,
+    g2m_live_h,
+    mesh_src_h,
+    mesh_dst_h,
+    out,
     mesh_feat,
     g2m_feat,
     g2m_rows,
@@ -52,7 +69,6 @@
     g2m_live,
     mesh_src,
     mesh_dst,
-    out,
     feat_v,
     gin_v,
     sec_v,
@@ -88,8 +104,14 @@
     far_lat = lat + 2 * par - 1
     has_far = jnp.logical_and(far_lat >= 0, far_lat < n_lat)
     far = (far_lat, lon)
-    lon_mates = [(lat, lax.rem(lon + t, n_lon)) for t in range(1, n_lon)]
-    x_mate = (lat + 2 - 4 * lax.rem(chip, 2), lon)
+    y = lax.rem(lon, 4)
+    diag_e, diag_w = (far_lat, east[1]), (far_lat, west[1])
+    is_y = [jnp.logical_and(has_far, y == k) for k in range(4)]
+    inner = jnp.logical_and(has_far, jnp.logical_or(y == 1, y == 2))
+    outer = jnp.logical_and(has_far, jnp.logical_or(y == 0, y == 3))
+    x_lat = lat + 2 - 4 * lax.rem(chip, 2)
+    plane_mates = [(lat, lax.rem(lon + t, n_lon)) for t in range(1, n_lon)]
+    plane_mates += [(x_lat, lax.rem(lon + t, n_lon)) for t in range(n_lon)]
     z_mates = [(lax.rem(lat + 4 * t, n_lat), lon) for t in range(1, n_lat // 4)]
 
     loads = {}
@@ -106,10 +128,31 @@
     load("feat", grid_feat, feat_v)
     load("gin", grid_in, gin_v)
     load("s0", second.at[0], sec_v.at[0])
+    load("gains", norm_gains_h, norm_gains)
     load("e0", edge_first.at[0], ef_v.at[0])
+    load("mesh_feat", mesh_feat_h, mesh_feat)
+    load("mesh_in", mesh_in_h, mesh_in)
     load("s1", second.at[1], sec_v.at[1])
     load("s2", second.at[2], sec_v.at[2])
+    load("edge_in", edge_in_h, edge_in)
+    for name, source, target in (
+        ("g2m_feat", g2m_feat_h, g2m_feat),
+        ("g2m_rows", g2m_rows_h, g2m_rows),
+        ("g2m_mask", g2m_mask_h, g2m_mask),
+        ("g2m_src", g2m_src_h, g2m_src),
+        ("g2m_dst", g2m_dst_h, g2m_dst),
+        ("g2m_live", g2m_live_h, g2m_live),
+    ):
+        load(name, source, target)
     load("n0", node_first.at[0], nf_v.at[0])
+    for name, source, target in (
+        ("mesh_efeat", mesh_efeat_h, mesh_efeat),
+        ("mesh_rows", mesh_rows_h, mesh_rows),
+        ("mesh_mask", mesh_mask_h, mesh_mask),
+        ("mesh_src", mesh_src_h, mesh_src),
+        ("mesh_dst", mesh_dst_h, mesh_dst),
+    ):
+        load(name, source, target)
     load("s3", second.at[3], sec_v.at[3])
     load("e1", edge_first.at[1], ef_v.at[1])
     load("s4", second.at[4], sec_v.at[4])
@@ -119,7 +162,7 @@
     load("s7", second.at[7], sec_v.at[7])
 
     barrier = pltpu.get_barrier_semaphore()
-    mates = lon_mates + [twin, x_mate] + z_mates
+    mates = plane_mates + [twin] + z_mates
     for mate in mates:
         pl.semaphore_signal(barrier, inc=1, device_id=mate, device_id_type=MESH)
 
@@ -127,10 +170,15 @@
     def _():
         pl.semaphore_signal(barrier, inc=1, device_id=far, device_id_type=MESH)
 
-    gains = norm_gains[...].astype(F32)
-
+    for needed, diag in ((is_y[3], diag_e), (is_y[0], diag_w)):
+
+        @pl.when(needed)
+        def _(diag=diag):
+            pl.semaphore_signal(barrier, inc=1, device_id=diag, device_id_type=MESH)
+
+    peers = jnp.where(has_far, 1, 0) + jnp.where(outer, 1, 0)
     def gain(k):
-        return gains[k : k + 1]
+        return norm_gains[...].astype(F32)[k : k + 1]
 
     def centre(k):
         w = sec_v[k].astype(F32)
@@ -138,12 +186,13 @@
 
     numbers = {}
 
-    def remote(name, src, dst, device):
+    def remote(name, src, dst, device, sender=None):
         index = numbers.setdefault(name, len(numbers))
+        leave = numbers.setdefault(sender or name, len(numbers))
         return pltpu.make_async_remote_copy(
             src_ref=src,
             dst_ref=dst,
-            send_sem=send_sem.at[index],
+            send_sem=send_sem.at[leave],
             recv_sem=recv_sem.at[index],
             device_id=device,
             device_id_type=MESH,
@@ -162,6 +211,10 @@
     g_copies["twin"] = remote("gtwin", g_at(g_rows[1], 1, 2), g_at(off_row, 1, 2), twin)
     g_copies["far_e"] = remote("gfe", g_at(off_row, 2), g_at(off_row, 0), east)
     g_copies["far_w"] = remote("gfw", g_at(off_row, 1), g_at(off_row, 3), west)
+    g_diag_e = remote("gfe", g_at(g_rows[0], 2), g_at(on_row, 0), diag_e, "gdiag")
+    g_side_w = remote("gfe", g_at(g_rows[0], 0), g_at(on_row, 0), far, "gside")
+    g_side_e = remote("gfw", g_at(g_rows[0], 3), g_at(on_row, 3), far, "gside")
+    g_diag_w = remote("gfw", g_at(g_rows[0], 1), g_at(on_row, 3), diag_w, "gdiag")
     g_copies["twin_e"] = remote("gte", g_at(g_rows[1], 0), g_at(off_row, 0), twin)
     g_copies["twin_w"] = remote("gtw", g_at(g_rows[1], 3), g_at(off_row, 3), twin)
 
@@ -170,7 +223,7 @@
         gt[pl.ds(off_row * 4, 4)] = jnp.zeros((4, BLK, 512), BF)
         mt[pl.ds(2 * par * 9, 9)] = jnp.zeros((9, BLK, 512), BF)
 
-    loaded("feat", "gin", "s0")
+    loaded("feat", "gin", "s0", "gains")
     centre(0)
     w_in = gin_v[...]
     for t in range(2):
@@ -182,18 +235,21 @@
         proj = mm(latent, ef_v[0, 512:1024]).astype(BF)
         gt[pl.ds(g_rows[t] * 4 + 1, 2)] = proj.reshape(2, BLK, 512)
         if t == 0:
-            pl.semaphore_wait(barrier, len(mates) + jnp.where(has_far, 1, 0))
+            pl.semaphore_wait(barrier, len(mates) + peers)
 
             @pl.when(has_far)
             def _():
                 g_copies["far"].start()
+
+            pl.when(is_y[3])(g_diag_e.start)
+            pl.when(is_y[0])(g_diag_w.start)
 
         else:
             g_copies["twin"].start()
         g_copies["e", t].start()
         g_copies["w", t].start()
 
-    loaded("s1")
+    loaded("s1", "mesh_feat", "mesh_in")
     centre(1)
     u = lax.dot_general(
         mesh_feat[0, 0], mesh_in[...], (((0,), (0,)), ((), ())), preferred_element_type=F32
@@ -225,9 +281,10 @@
             pick_s = jnp.where(spot == hs, 1.0, 0.0).T.astype(BF)
             pick_d = jnp.where(spot == hd, 1.0, 0.0).T.astype(BF)
             pick[s] = jnp.concatenate([pick_s, pick_d], axis=1)
-            keep = mask[0, 0, pl.ds(s, 1), :]
-            if live is not None:
-                keep = keep * jnp.where(s < live, 1, 0)
+            if live is None:
+                keep = mask[0, 0, pl.ds(s, 1), :]
+            else:
+                keep = mask[0, s] * jnp.where(s < live, 1, 0)
             target = jnp.where(keep != 0, hd + BLK * dst[0, 0, s], -1)
             one = jnp.where(place == target, 1.0, 0.0).astype(BF)
             scat[s] = one
@@ -251,8 +308,8 @@
     acc_m[...] = zeros
     acc_g[...] = zeros
     acc_h[...] = zeros
+    loaded("s2", "edge_in", "g2m_feat", "g2m_rows", "g2m_mask", "g2m_src", "g2m_dst", "g2m_live")
     live = g2m_live[0, 0]
-    loaded("s2")
     centre(2)
 
     @pl.loop(0, 6 // GGROUP)
@@ -262,18 +319,15 @@
             0, 2, g_pre, g_pick, g_scat, acc_g, False,
         )
 
-    @pl.when(has_far)
-    def _():
-        g_copies["far"].wait_recv()
-        g_copies["far_e"].start()
-        g_copies["far_w"].start()
-
-    g_copies["e", 1].wait_recv()
-    g_copies["twin_e"].start()
-    g_copies["w", 1].wait_recv()
-    g_copies["twin_w"].start()
-
-    loaded("s3", "e1")
+    pl.when(has_far)(g_copies["far"].wait_recv)
+    pl.when(inner)(g_copies["far_e"].start)
+    pl.when(inner)(g_copies["far_w"].start)
+    pl.when(y == 1)(g_copies["e", 0].wait_recv)
+    pl.when(is_y[1])(g_side_w.start)
+    pl.when(y == 2)(g_copies["w", 0].wait_recv)
+    pl.when(is_y[2])(g_side_e.start)
+
+    loaded("s3", "e1", "mesh_efeat", "mesh_rows", "mesh_mask", "mesh_src", "mesh_dst")
     centre(3)
 
     def embed_mesh(n):
@@ -290,7 +344,13 @@
     for k in (4, 6, 5, 7):
         centre(k)
 
-    for name in (("e", 0), ("w", 0), "twin", "twin_e", "twin_w"):
+    g_copies["e", 1].wait_recv()
+    g_copies["twin_e"].start()
+    g_copies["w", 1].wait_recv()
+    g_copies["twin_w"].start()
+    pl.when(y != 1)(g_copies["e", 0].wait_recv)
+    pl.when(y != 2)(g_copies["w", 0].wait_recv)
+    for name in ("twin", "twin_e", "twin_w"):
         g_copies[name].wait_recv()
 
     @pl.when(has_far)
@@ -317,15 +377,39 @@
         m_copies["twin_e", b] = remote(("mte", b), m_at(1, 0, b), m_at(m_off, 0, b), twin)
         m_copies["twin_w", b] = remote(("mtw", b), m_at(1, 2, b), m_at(m_off, 2, b), twin)
 
+    m_diag_e = [remote(("mfe", b), m_at(1, 1, b), m_at(m_on, 0, b), diag_e, ("md", b)) for b in range(3)]
+    m_side_w = [remote(("mfe", b), m_at(1, 0, b), m_at(m_on, 0, b), far, ("ms", b)) for b in range(3)]
+    m_side_e = [remote(("mfw", b), m_at(1, 2, b), m_at(m_on, 2, b), far, ("ms", b)) for b in range(3)]
+    m_diag_w = [remote(("mfw", b), m_at(1, 1, b), m_at(m_on, 2, b), diag_w, ("md", b)) for b in range(3)]
+
     half = pl.ds(pl.multiple_of(par * 256, 256), 256)
     unit = mt.at[NEAR + chip, pl.ds(pl.multiple_of(lon * 16, 16), 16), half]
-    c_lon = [remote(("cl", t), unit, unit, mate) for t, mate in enumerate(lon_mates)]
-    line = mt.at[NEAR + chip, :, half]
-    c_x = remote("cx", line, line, x_mate)
-    plane = mt.at[pl.ds(NEAR + 2 * (chip // 2), 2), :, half]
-    c_z = [remote(("cz", t), plane, plane, mate) for t, mate in enumerate(z_mates)]
-    cube = mt.at[pl.ds(NEAR, 8), :, half]
-    c_core = remote("cc", cube, cube, twin)
+    c_unit = [remote(("cu", t), unit, unit, mate) for t, mate in enumerate(plane_mates)]
+    z = chip // 2
+
+    def plane(t):
+        return mt.at[pl.ds(NEAR + 2 * lax.rem(z + t, 4), 2), :, half]
+
+    c_z = [remote(("cz", t), plane(0), plane(0), mate) for t, mate in enumerate(z_mates)]
+    c_twin = [remote(("cc", t), plane(t), plane(t), twin) for t in range(4)]
+
+    def coarse_out():
+        m_copies["twin", 0].wait_recv()
+        mine = mt[12, 0:16].astype(F32)[0:COARSE]
+        other = mt[(m_on * 3 + 1) * 3, 0:16].astype(F32)[0:COARSE]
+        top = jnp.where(par == 0, mine, other)
+        low = jnp.where(par == 0, other, mine)
+        both = jnp.concatenate([top, low], axis=0)
+        unit[...] = jnp.where(par == 0, both[:, 0:256], both[:, 256:512]).astype(BF)
+        for copy in c_unit:
+            copy.start()
+
+    def patch_out(b):
+        pl.when(has_far)(m_copies["far", b].start)
+        pl.when(is_y[3])(m_diag_e[b].start)
+        pl.when(is_y[0])(m_diag_w[b].start)
+        m_copies["e", b].start()
+        m_copies["w", b].start()
 
     g2m_round = (acc_g[...] + acc_h[...] * gain(4)).astype(BF)
     node_w = nf_v[0, 512:1024]
@@ -337,96 +421,84 @@
         one_v[rows] = one
         mt[12 + b] = mm(one, ef_v[1, 512:1024]).astype(BF)
 
-        @pl.when(has_far)
-        def _(b=b):
-            m_copies["far", b].start()
-
-        for name in ("e", "w", "twin"):
-            m_copies[name, b].start()
+        m_copies["twin", b].start()
+        if b == 1:
+            coarse_out()
+            patch_out(0)
+        if b >= 1:
+            patch_out(b)
 
     one = one_v[...]
     dproj[...] = mm(one, ef_v[1, 1024:1536]).astype(BF).reshape(3, BLK, 512)
-    m_copies["twin", 0].wait_recv()
-    mine = mt[12, 0:16].astype(F32)[0:COARSE]
-    other = mt[(m_on * 3 + 1) * 3, 0:16].astype(F32)[0:COARSE]
-    top = jnp.where(par == 0, mine, other)
-    low = jnp.where(par == 0, other, mine)
-    both = jnp.concatenate([top, low], axis=0)
-    unit[...] = jnp.where(par == 0, both[:, 0:256], both[:, 256:512]).astype(BF)
-    for copy in c_lon:
-        copy.start()
     npre[...] = mm(one, nf_v[1, 0:512])
 
-    def forward(b):
-        @pl.when(has_far)
-        def _():
-            m_copies["far", b].wait_recv()
-            m_copies["far_e", b].start()
-            m_copies["far_w", b].start()
-
-        m_copies["e", b].wait_recv()
-        m_copies["twin_e", b].start()
-        m_copies["w", b].wait_recv()
-        m_copies["twin_w", b].start()
+    def corners(b):
+        pl.when(has_far)(m_copies["far", b].wait_recv)
+        pl.when(inner)(m_copies["far_e", b].start)
+        pl.when(inner)(m_copies["far_w", b].start)
+        pl.when(y == 1)(m_copies["e", b].wait_recv)
+        pl.when(is_y[1])(m_side_w[b].start)
+        pl.when(y == 2)(m_copies["w", b].wait_recv)
+        pl.when(is_y[2])(m_side_e[b].start)
 
     groups = 24 // GROUP
-    late = groups - EARLY
-
-    @pl.loop(EARLY, EARLY + late // 4)
-    def _(n):
-        embed_mesh(n)
-
-    for copy in c_lon:
+
+    pl.loop(EARLY, EARLY + 2)(embed_mesh)
+    for copy in c_unit:
         copy.wait_recv()
-    c_x.start()
-    forward(0)
-
-    @pl.loop(EARLY + late // 4, EARLY + late // 2)
-    def _(n):
-        embed_mesh(n)
-
-    c_x.wait_recv()
-    for copy in c_z:
-        copy.start()
-    forward(1)
-
-    @pl.loop(EARLY + late // 2, groups)
-    def _(n):
-        embed_mesh(n)
-
-    forward(2)
-    for copy in c_z:
-        copy.wait_recv()
-    c_core.start()
+    for t in (0, 2, 1):
+        c_z[t].start()
+    c_twin[0].start()
+    pl.when(inner)(functools.partial(corners, 0))
+    pl.loop(EARLY + 2, EARLY + 3)(embed_mesh)
+    pl.when(inner)(functools.partial(corners, 1))
+    pl.loop(EARLY + 3, groups)(embed_mesh)
+    pl.when(inner)(functools.partial(corners, 2))
+    for t in (0, 2, 1):
+        c_z[t].wait_recv()
+        c_twin[3 - t].start()
     for b in range(3):
+        @pl.when(jnp.logical_not(inner))
+        def _(b=b):
+            corners(b)
+
         if b:
             m_copies["twin", b].wait_recv()
+        pl.when(y != 1)(m_copies["e", b].wait_recv)
+        m_copies["twin_e", b].start()
+        pl.when(y != 2)(m_copies["w", b].wait_recv)
+        m_copies["twin_w", b].start()
+    for b in range(3):
         m_copies["twin_e", b].wait_recv()
         m_copies["twin_w", b].wait_recv()
-
-        @pl.when(has_far)
-        def _(b=b):
-            m_copies["far_e", b].wait_recv()
-            m_copies["far_w", b].wait_recv()
-
-    c_core.wait_recv()
-
-    @pl.loop(0, groups)
+        pl.when(has_far)(m_copies["far_e", b].wait_recv)
+        pl.when(has_far)(m_copies["far_w", b].wait_recv)
+    for copy in c_twin:
+        copy.wait_recv()
+
+    @pl.loop(0, 24 // UGROUP)
     def _(n):
-        update(n * GROUP, GROUP, mesh_src, mesh_dst, 5, m_pre, m_pick, m_scat, mt, acc_m)
+        update(n * UGROUP, UGROUP, mesh_src, mesh_dst, 5, m_pre, m_pick, m_scat, mt, acc_m)
 
     mesh_round = (acc_e[...] + acc_m[...] * gain(5)).astype(BF)
     u = npre[...] + mm(mesh_round, nf_v[1, 512:1024])
     step = unit_rows(mm(silu(u), sec_v[7])) * gain(7)
     out[0, 0] = (one_v[...].astype(F32) + step).astype(BF)
 
+    pl.when(outer)(g_diag_e.wait_send)
+    pl.when(inner)(g_side_e.wait_send)
+    for b in range(3):
+        pl.when(outer)(m_diag_e[b].wait_send)
+        pl.when(inner)(m_side_e[b].wait_send)
     for name, copy in list(g_copies.items()) + list(m_copies.items()):
         kind = name if isinstance(name, str) else name[0]
-        if kind.startswith("far"):
+        if kind == "far":
             pl.when(has_far)(copy.wait_send)
+        elif kind.startswith("far"):
+            pl.when(inner)(copy.wait_send)
         else:
             copy.wait_send()
-    for copy in c_lon + [c_x] + c_z + [c_core]:
+    for copy in c_unit + c_z + c_twin:
         copy.wait_send()
 
 
@@ -454,14 +526,29 @@
 ):
     hbm = pl.BlockSpec(memory_space=pl.ANY)
     vmem = pl.BlockSpec(memory_space=pltpu.VMEM)
-    smem = pl.BlockSpec(memory_space=pltpu.SMEM)
+    g2m_mask = jnp.swapaxes(g2m_mask, 1, 2)
+    small = (
+        mesh_feat,
+        g2m_feat,
+        g2m_rows,
+        g2m_mask,
+        mesh_efeat,
+        mesh_rows,
+        mesh_mask,
+        mesh_in,
+        edge_in,
+        norm_gains,
+    )
+    scalars = (g2m_src, g2m_dst, g2m_live, mesh_src, mesh_dst)
     copies = 96
     return pl.pallas_call(
         kernel,
         out_shape=jax.ShapeDtypeStruct((1, 1, 384, 512), BF),
-        in_specs=[hbm] * 5 + [vmem] * 10 + [smem] * 5,
+        in_specs=[hbm] * 20,
         out_specs=vmem,
-        scratch_shapes=[
+        scratch_shapes=[pltpu.VMEM(x.shape, x.dtype) for x in small]
+        + [pltpu.SMEM(x.shape, x.dtype) for x in scalars]
+        + [
             pltpu.VMEM((2, 2, BLK, 474), BF),
             pltpu.VMEM((474, 512), BF),
             pltpu.VMEM((8, 512, 512), BF),
@@ -483,7 +570,7 @@
             pltpu.VMEM((384, 512), F32),
             pltpu.VMEM((384, 512), F32),
             pltpu.VMEM((384, 512), F32),
-            pltpu.SemaphoreType.DMA((14,)),
+            pltpu.SemaphoreType.DMA((32,)),
             pltpu.SemaphoreType.DMA((copies,)),
             pltpu.SemaphoreType.DMA((copies,)),
         ],
@@ -497,21 +584,8 @@
         second,
         edge_first,
         node_first,
-        mesh_feat,
-        g2m_feat,
-        g2m_rows,
-        g2m_mask,
-        mesh_efeat,
-        mesh_rows,
-        mesh_mask,
-        mesh_in,
-        edge_in,
-        norm_gains,
-        g2m_src,
-        g2m_dst,
-        g2m_live,
-        mesh_src,
-        mesh_dst,
+        *small,
+        *scalars,
     )
 
 

time: 76.6 us -> 65.9 us (0.86)
  Pallas kernels: 70.7 us -> 61.1 us
  local copies, waits for them, and re-layouts: 5.02 us -> 3.75 us
    pallas_call x1, Pallas kernels: 70.7 us -> 61.1 us  [per_device(): pl.pallas_call(kernel, out_shape=jax.ShapeDtypeStruct((1, 1, 384, 512), B...]
    unnamed x3 -> x2, local copies, waits for them, and re-layouts: 5.02 us -> 3.75 us
where the time goes in v2:
time: 65.9 us; the launch traced here: 65.6 us
  Pallas kernels  61.1 us (93%)
  local copies, waits for them, and re-layouts  3.75 us (6%)
  between operations  0.66 us (1%)
    pallas_call x1, Pallas kernels, per_device(): pl.pallas_call(kernel, out_shape=jax.ShapeDtypeStruct((1, 1, 384, 512), B...  61.1 us
    unnamed x2, local copies, waits for them, and re-layouts  3.75 us

profile of v2, /device:TPU:1, one launch (start us, length us, event | category | flops | bytes accessed | tf_op | source)
XLA Modules:
  0.0 65.6 jit_solution(17868563958740237129)
XLA Ops:
  0.7 2.0 %copy.21.grid_feat = bf16[2,2,128,474]{3,2,1,0:T(8,128)(2,1)} copy(bf16[2,2,128,474]{2,1,3,0:T(2,128)(2,1)} %param.20) | data formatting | bytes 970752 | tf_op args[0]
  2.6 61.1 %shard_map.190 = bf16[1,1,384,512]{3,2,1,0:T(8,128)(2,1)} custom-call(bf16[2,2,128,474]{3,2,1,0:T(8,128)(2,1)} %copy.21.grid_feat, bf16[474,512]{1,0:T(8,128)(2,1)} %grid_in.1, bf16[8,512,512]{2,1,0:T(8,128)(2,1)} %second.1, bf16[2,1536,512]{2,1,0:T(8,128)(2,1)} %edge_first.1, bf16[2,1024,512]{2,1,0:T(8,128)(2,1)} %node_first.1, ...), custom_call_target="tpu_custom_call" | custom-call | flops 12999999488 | bytes 12582912 | tf_op jit(solution)/shard_map/pallas_call | solution.py:544
  63.8 1.8 %copy.24 = bf16[1,1,384,512]{3,2,1,0:T(8,128)(2,1)} copy(bf16[1,1,384,512]{3,2,1,0:T(8,128)(2,1)} %shard_map.190) | data formatting | bytes 786432

commit v3 on v2

--- a/solution.py
+++ b/solution.py
@@ -12,7 +12,7 @@
 MESH = pl.DeviceIdType.MESH
 BLK = 128
 GROUP = 4
-UGROUP = 8
+UGROUP = 12
 GGROUP = 6
 EARLY = 2
 NEAR = 27
@@ -454,9 +454,6 @@
     pl.when(inner)(functools.partial(corners, 1))
     pl.loop(EARLY + 3, groups)(embed_mesh)
     pl.when(inner)(functools.partial(corners, 2))
-    for t in (0, 2, 1):
-        c_z[t].wait_recv()
-        c_twin[3 - t].start()
     for b in range(3):
         @pl.when(jnp.logical_not(inner))
         def _(b=b):
@@ -468,6 +465,9 @@
         m_copies["twin_e", b].start()
         pl.when(y != 2)(m_copies["w", b].wait_recv)
         m_copies["twin_w", b].start()
+    for t in (0, 2, 1):
+        c_z[t].wait_recv()
+        c_twin[3 - t].start()
     for b in range(3):
         m_copies["twin_e", b].wait_recv()
         m_copies["twin_w", b].wait_recv()

time: 65.9 us -> 64.5 us (0.979)
  Pallas kernels: 61.1 us -> 59.8 us
    pallas_call x1, Pallas kernels: 61.1 us -> 59.8 us  [per_device(): pl.pallas_call(kernel, out_shape=jax.ShapeDtypeStruct((1, 1, 384, 512), B...]
where the time goes in v3:
time: 64.5 us; the launch traced here: 64.2 us
  Pallas kernels  59.8 us (93%)
  local copies, waits for them, and re-layouts  3.75 us (6%)
  between operations  0.66 us (1%)
    pallas_call x1, Pallas kernels, per_device(): pl.pallas_call(kernel, out_shape=jax.ShapeDtypeStruct((1, 1, 384, 512), B...  59.8 us
    unnamed x2, local copies, waits for them, and re-layouts  3.75 us

profile of v3, /device:TPU:1, one launch (start us, length us, event | category | flops | bytes accessed | tf_op | source)
XLA Modules:
  0.0 64.2 jit_solution(805962619061746069)
XLA Ops:
  0.7 2.0 %copy.21.grid_feat = bf16[2,2,128,474]{3,2,1,0:T(8,128)(2,1)} copy(bf16[2,2,128,474]{2,1,3,0:T(2,128)(2,1)} %param.20) | data formatting | bytes 970752 | tf_op args[0]
  2.6 59.8 %shard_map.190 = bf16[1,1,384,512]{3,2,1,0:T(8,128)(2,1)} custom-call(bf16[2,2,128,474]{3,2,1,0:T(8,128)(2,1)} %copy.21.grid_feat, bf16[474,512]{1,0:T(8,128)(2,1)} %grid_in.1, bf16[8,512,512]{2,1,0:T(8,128)(2,1)} %second.1, bf16[2,1536,512]{2,1,0:T(8,128)(2,1)} %edge_first.1, bf16[2,1024,512]{2,1,0:T(8,128)(2,1)} %node_first.1, ...), custom_call_target="tpu_custom_call" | custom-call | flops 12999999488 | bytes 12582912 | tf_op jit(solution)/shard_map/pallas_call | solution.py:544
  62.4 1.8 %copy.24 = bf16[1,1,384,512]{3,2,1,0:T(8,128)(2,1)} copy(bf16[1,1,384,512]{3,2,1,0:T(8,128)(2,1)} %shard_map.190) | data formatting | bytes 786432

commit v4 on v3

--- a/solution.py
+++ b/solution.py
@@ -129,7 +129,25 @@
     load("gin", grid_in, gin_v)
     load("s0", second.at[0], sec_v.at[0])
     load("gains", norm_gains_h, norm_gains)
-    load("e0", edge_first.at[0], ef_v.at[0])
+    load("e0s", edge_first.at[0, pl.ds(512, 512)], ef_v.at[0, pl.ds(512, 512)])
+
+    barrier = pltpu.get_barrier_semaphore()
+    mates = plane_mates + [twin] + z_mates
+    for mate in mates:
+        pl.semaphore_signal(barrier, inc=1, device_id=mate, device_id_type=MESH)
+
+    @pl.when(has_far)
+    def _():
+        pl.semaphore_signal(barrier, inc=1, device_id=far, device_id_type=MESH)
+
+    for needed, diag in ((is_y[3], diag_e), (is_y[0], diag_w)):
+
+        @pl.when(needed)
+        def _(diag=diag):
+            pl.semaphore_signal(barrier, inc=1, device_id=diag, device_id_type=MESH)
+
+    load("e0d", edge_first.at[0, pl.ds(1024, 512)], ef_v.at[0, pl.ds(1024, 512)])
+    load("e0e", edge_first.at[0, pl.ds(0, 512)], ef_v.at[0, pl.ds(0, 512)])
     load("mesh_feat", mesh_feat_h, mesh_feat)
     load("mesh_in", mesh_in_h, mesh_in)
     load("s1", second.at[1], sec_v.at[1])
@@ -161,21 +179,6 @@
     load("n1", node_first.at[1], nf_v.at[1])
     load("s7", second.at[7], sec_v.at[7])
 
-    barrier = pltpu.get_barrier_semaphore()
-    mates = plane_mates + [twin] + z_mates
-    for mate in mates:
-        pl.semaphore_signal(barrier, inc=1, device_id=mate, device_id_type=MESH)
-
-    @pl.when(has_far)
-    def _():
-        pl.semaphore_signal(barrier, inc=1, device_id=far, device_id_type=MESH)
-
-    for needed, diag in ((is_y[3], diag_e), (is_y[0], diag_w)):
-
-        @pl.when(needed)
-        def _(diag=diag):
-            pl.semaphore_signal(barrier, inc=1, device_id=diag, device_id_type=MESH)
-
     peers = jnp.where(has_far, 1, 0) + jnp.where(outer, 1, 0)
     def gain(k):
         return norm_gains[...].astype(F32)[k : k + 1]
@@ -231,7 +234,7 @@
         v = mm(silu(mm(x, w_in)), sec_v[0])
         latent = (unit_rows(v) * gain(0)).astype(BF)
         if t == 0:
-            loaded("e0")
+            loaded("e0s")
         proj = mm(latent, ef_v[0, 512:1024]).astype(BF)
         gt[pl.ds(g_rows[t] * 4 + 1, 2)] = proj.reshape(2, BLK, 512)
         if t == 0:
@@ -249,7 +252,7 @@
         g_copies["e", t].start()
         g_copies["w", t].start()
 
-    loaded("s1", "mesh_feat", "mesh_in")
+    loaded("s1", "mesh_feat", "mesh_in", "e0d", "e0e")
     centre(1)
     u = lax.dot_general(
         mesh_feat[0, 0], mesh_in[...], (((0,), (0,)), ((), ())), preferred_element_type=F32

time: 64.5 us -> 64.6 us (level)
  no operation moved by 1% of the time
where the time goes in v4:
time: 64.6 us; the launch traced here: 64.1 us
  Pallas kernels  59.7 us (92%)
  local copies, waits for them, and re-layouts  3.75 us (6%)
  between operations  0.66 us (1%)
    pallas_call x1, Pallas kernels, per_device(): pl.pallas_call(kernel, out_shape=jax.ShapeDtypeStruct((1, 1, 384, 512), B...  59.7 us
    unnamed x2, local copies, waits for them, and re-layouts  3.75 us

profile of v4, /device:TPU:1, one launch (start us, length us, event | category | flops | bytes accessed | tf_op | source)
XLA Modules:
  0.0 64.1 jit_solution(12276742394416107655)
XLA Ops:
  0.7 2.0 %copy.21.grid_feat = bf16[2,2,128,474]{3,2,1,0:T(8,128)(2,1)} copy(bf16[2,2,128,474]{2,1,3,0:T(2,128)(2,1)} %param.20) | data formatting | bytes 970752 | tf_op args[0]
  2.6 59.7 %shard_map.190 = bf16[1,1,384,512]{3,2,1,0:T(8,128)(2,1)} custom-call(bf16[2,2,128,474]{3,2,1,0:T(8,128)(2,1)} %copy.21.grid_feat, bf16[474,512]{1,0:T(8,128)(2,1)} %grid_in.1, bf16[8,512,512]{2,1,0:T(8,128)(2,1)} %second.1, bf16[2,1536,512]{2,1,0:T(8,128)(2,1)} %edge_first.1, bf16[2,1024,512]{2,1,0:T(8,128)(2,1)} %node_first.1, ...), custom_call_target="tpu_custom_call" | custom-call | flops 12999999488 | bytes 12582912 | tf_op jit(solution)/shard_map/pallas_call | solution.py:547
  62.3 1.8 %copy.24 = bf16[1,1,384,512]{3,2,1,0:T(8,128)(2,1)} copy(bf16[1,1,384,512]{3,2,1,0:T(8,128)(2,1)} %shard_map.190) | data formatting | bytes 786432
